TPU v7x, 32 devices: a whole 2x2x4 slice. The times are simulated.
32 devices in a mesh: sec: 4 (over x, core), ctx: 8 (over z, y).
Axes of the slice: x: 2, y: 2, z: 4, core: 2. Of those that a mesh axis runs over, the one named last changes fastest.
Arguments:
- queries: bfloat16 [4, 16, 64, 4096], P('sec', 'ctx'), may hold values from -6 to 6
- head_weights: float32 [4, 16, 64, 32], P('sec', 'ctx'), may hold values from -0.9 to 0.9
- key_vectors: bfloat16 [4, 65536, 128], P('sec', 'ctx'), may hold values from -6 to 6
- targets: bfloat16 [4, 16, 64, 4096], P('sec', 'ctx'), may hold values from 0 to 0.0019989014
- normalizers: float32 [4, 16, 64], P('sec', 'ctx'), may hold values from 7 to 9
- loss_grad: float32 [4, 16, 64], P('sec', 'ctx'), may hold values from 300 to 3000
- tile_slot: int32 [4, 16], P('sec', 'ctx'), may hold values from 0 to 127
- doc_start: int32 [4, 16], P('sec', 'ctx'), may hold values from 0 to 65535, as said below
Outputs:
- queries_grad: bfloat16 [4, 16, 64, 4096], P('sec', 'ctx')
- weights_grad: float32 [4, 16, 64, 32], P('sec', 'ctx')
- key_grads: bfloat16 [4, 65536, 128], P('sec', 'ctx')
Inputs may be any that keep to these rules, and one draw needn't show every extreme that they name: `doc_start`: qpos of every task lies in its device's positions; the document of a task starts at or before its first query and spans 1 to 4 key blocks up to its last query; the first task of every device but the first spans 4 blocks and its document starts on the device before.
All inputs are finite; a program needn't handle non-finite values.
Results may differ from a plain program's by a relative error of at most 0.0051.
Values may be sent and summed in bfloat16 or wider, within the bound.
No kernel may reach another device: no remote copies, remote signals or barrier semaphores. Data moves between devices by JAX's collectives and lax.ppermute only.
A program may use at most 192 MiB of HBM per device.

v0:
```python
import jax
import jax.numpy as jnp
from jax import lax
from jax.sharding import PartitionSpec as P

BLK = 1024
MAXB = 4
QT = 64
KB_DEV = 8


def passed_along(array, axis, by):
    size = lax.axis_size(axis)
    pairs = [(i, i + by) for i in range(size) if 0 <= i + by < size]
    return lax.ppermute(array, axis, pairs)


def block_terms(
    query_rows,
    weight_rows,
    normalizer,
    cotangent,
    target_block,
    key_block,
    key_first,
    query_pos,
    doc_begin,
    inside,
):
    tile_rows = weight_rows.shape[0]
    head_count = weight_rows.shape[1]
    block_width = key_block.shape[0]
    factor = 1.0 / key_block.shape[1] ** 0.5
    scores = lax.dot_general(
        query_rows, key_block, (((1,), (1,)), ((), ())), preferred_element_type=jnp.float32
    )
    scores = scores.reshape(tile_rows, head_count, block_width)
    active = jnp.maximum(scores, 0.0) * factor
    index_value = jnp.sum(weight_rows[:, :, None] * active, axis=1)
    key_pos = key_first + jnp.arange(block_width, dtype=jnp.int32)
    live = (key_pos[None, :] >= doc_begin) & (key_pos[None, :] <= query_pos[:, None]) & inside
    delta = jnp.where(
        live,
        cotangent[:, None]
        * (jnp.exp(index_value - normalizer[:, None]) - target_block.astype(jnp.float32)),
        0.0,
    )
    weight_part = jnp.sum(delta[:, None, :] * active, axis=2)
    score_grad = jnp.where(
        scores > 0, delta[:, None, :] * weight_rows[:, :, None] * factor, 0.0
    ).astype(jnp.bfloat16)
    score_grad = score_grad.reshape(tile_rows * head_count, block_width)
    query_part = jnp.dot(score_grad, key_block, preferred_element_type=jnp.float32)
    key_part = lax.dot_general(
        score_grad, query_rows, (((0,), (0,)), ((), ())), preferred_element_type=jnp.float32
    )
    return (query_part, weight_part, key_part)


def run_task(
    query_tile,
    weight_rows,
    target_rows,
    normalizer,
    cotangent,
    query_first,
    doc_begin,
    avail_keys,
    avail_first,
    avail_blocks,
    key_padded,
):
    depth = avail_keys.shape[1]
    tile_rows = weight_rows.shape[0]
    head_count = weight_rows.shape[1]
    query_rows = query_tile.reshape(tile_rows * head_count, depth)
    query_pos = query_first + jnp.arange(tile_rows, dtype=jnp.int32)
    slot_limit = target_rows.shape[1] // BLK
    first_block = doc_begin // BLK
    block_count = (query_first + tile_rows - 1) // BLK - first_block + 1
    lower = jnp.maximum(0, avail_first - first_block)
    upper = jnp.minimum(
        jnp.minimum(block_count, slot_limit), avail_first + avail_blocks - first_block
    )

    def per_slot(slot_index, carry):
        query_total, weight_total, slot_sums = carry
        block_id = first_block + slot_index
        inside = (
            (slot_index < block_count)
            & (slot_index < slot_limit)
            & (block_id >= avail_first)
            & (block_id < avail_first + avail_blocks)
        )
        local_block = jnp.clip(block_id - avail_first, 0, avail_blocks - 1)
        key_block = lax.dynamic_slice_in_dim(avail_keys, local_block * BLK, BLK, 0)
        target_block = lax.dynamic_slice_in_dim(
            target_rows, jnp.minimum(slot_index, slot_limit - 1) * BLK, BLK, 1
        )
        query_part, weight_part, key_part = block_terms(
            query_rows,
            weight_rows,
            normalizer,
            cotangent,
            target_block,
            key_block,
            block_id * BLK,
            query_pos,
            doc_begin,
            inside,
        )
        slot_sums = lax.dynamic_update_slice_in_dim(slot_sums, key_part, slot_index * BLK, 0)
        return (query_total + query_part, weight_total + weight_part, slot_sums)

    start_state = (
        jnp.zeros((tile_rows * head_count, depth), jnp.float32),
        jnp.zeros((tile_rows, head_count), jnp.float32),
        jnp.zeros((MAXB * BLK, depth), jnp.float32),
    )
    query_total, weight_total, slot_sums = lax.fori_loop(lower, upper, per_slot, start_state)
    window_start = jnp.clip(first_block - avail_first + MAXB, 0, avail_blocks + MAXB) * BLK
    previous = lax.dynamic_slice_in_dim(key_padded, window_start, MAXB * BLK, 0)
    key_padded = lax.dynamic_update_slice_in_dim(key_padded, previous + slot_sums, window_start, 0)
    return (query_total.reshape(tile_rows, head_count * depth), weight_total, key_padded)


def local(
    queries, head_weights, key_vectors, targets, normalizers, loss_grad, tile_slot, doc_start
):
    ctx_index = lax.axis_index("ctx")
    dev_first = ctx_index * KB_DEV
    local_keys = key_vectors[0]
    depth = local_keys.shape[1]
    rim_blocks = MAXB - 1
    task_total = queries.shape[1]
    own_first = dev_first * BLK + tile_slot[0] * QT
    query_list = []
    weight_list = []
    rim_keys = passed_along(local_keys[(KB_DEV - rim_blocks) * BLK :], "ctx", 1)
    avail_keys = jnp.concatenate([rim_keys, local_keys], axis=0)
    avail_blocks = KB_DEV + rim_blocks
    key_padded = jnp.zeros(((avail_blocks + 2 * MAXB) * BLK, depth), jnp.float32)
    for task_index in range(task_total):
        query_part, weight_part, key_padded = run_task(
            queries[0, task_index],
            head_weights[0, task_index],
            targets[0, task_index],
            normalizers[0, task_index],
            loss_grad[0, task_index],
            own_first[task_index],
            doc_start[0, task_index],
            avail_keys,
            dev_first - rim_blocks,
            avail_blocks,
            key_padded,
        )
        query_list.append(query_part)
        weight_list.append(weight_part)
    key_total = key_padded[MAXB * BLK : (MAXB + avail_blocks) * BLK]
    returned = passed_along(key_total[: rim_blocks * BLK].astype(jnp.bfloat16), "ctx", -1)
    key_own = key_total[rim_blocks * BLK :]
    key_own = jnp.concatenate(
        [
            key_own[: (KB_DEV - rim_blocks) * BLK],
            key_own[(KB_DEV - rim_blocks) * BLK :] + returned.astype(jnp.float32),
        ],
        axis=0,
    )
    query_out = jnp.stack(query_list).astype(jnp.bfloat16)[None]
    weight_out = jnp.stack(weight_list)[None]
    key_out = key_own.astype(jnp.bfloat16)[None]
    return (query_out, weight_out, key_out)


def solution(mesh):
    return jax.shard_map(
        local,
        mesh=mesh,
        in_specs=(
            P("sec", "ctx", None, None),
            P("sec", "ctx", None, None),
            P("sec", "ctx", None),
            P("sec", "ctx", None, None),
            P("sec", "ctx", None),
            P("sec", "ctx", None),
            P("sec", "ctx"),
            P("sec", "ctx"),
        ),
        out_specs=(P("sec", "ctx", None, None), P("sec", "ctx", None, None), P("sec", "ctx", None)),
        check_vma=False,
    )
```

profile of v0, /device:TPU:22, one launch (start us, length us, event | category | flops | bytes accessed | tf_op | source)
XLA Modules:
  0.0 624.9 jit_solution(3012243121424256623)
XLA Ops:
  29.3 139.9 %while.35 = (s32[]{:T(128)}, f32[2048,128]{1,0:T(8,128)S(1)}, f32[64,32]{1,0:T(8,128)S(1)}, f32[4096,128]{1,0:T(8,128)}, s32[]{:T(128)}, /*index=5*/s32[]{:T(128...) while((s32[]{:T(128)}, f32[2048,128]{1,0:T(8,128)S(1)}, ...), condition=%wide.wide.region_7.8_spmd.clone, body=%wide.wide.region_4.7_spmd.clone.sunk | while | flops 1634472960 | bytes 194735712 | solution.py:120
  36.1 4.1 maximum_bitcast_fusion.8
  40.2 9.3 %copy.44 = f32[2048,1024]{1,0:T(8,128)} copy(f32[2048,1024]{0,1:T(8,128)} %maximum_bitcast_fusion.8) | data formatting | bytes 16777216 | tf_op jit(solution)/shard_map/while/body/max | solution.py:38
  49.5 4.8 multiply_reduce_fusion.14
  54.4 4.3 mul.347
  58.8 9.1 %copy.45 = f32[2048,1024]{0,1:T(8,128)} copy(f32[2048,1024]{1,0:T(8,128)} %bitcast.135) | data formatting | bytes 16777216 | tf_op jit(solution)/shard_map/while/body/mul | solution.py:48
  67.9 4.3 mul.348
  72.2 9.2 %copy.46 = f32[2048,1024]{0,1:T(8,128)} copy(f32[2048,1024]{1,0:T(8,128)} %bitcast.136) | data formatting | bytes 16777216 | tf_op jit(solution)/shard_map/while/body/mul | solution.py:50
  81.3 12.0 %multiply_reduce_fusion.15 = (f32[2048]{0:T(1024)S(1)}, bf16[2048,1024]{0,1:T(8,128)(2,1)}) fusion(f32[2048,1024]{0,1:T(8,128)} %copy.45, f32[1024,2048]{1,0:T(8,128)} %copy-done, f32[2048,1024]{0,1:T(8,128)} %copy.46, f32[2048]{0:T(1024)S(1)} %get-tuple-element.938), kind=kLoop, calls=%fused_computation.19.clone.clone.1 | loop fusion | flops 16775168 | bytes 29376512 | tf_op jit(solution)/shard_map/while/body/reduce_sum | solution.py:48
  110.0 9.3 %copy.44 = f32[2048,1024]{1,0:T(8,128)} copy(f32[2048,1024]{0,1:T(8,128)} %maximum_bitcast_fusion.8) | data formatting | bytes 16777216 | tf_op jit(solution)/shard_map/while/body/max | solution.py:38
  119.3 4.8 multiply_reduce_fusion.14
  124.3 4.3 mul.347
  128.6 9.1 %copy.45 = f32[2048,1024]{0,1:T(8,128)} copy(f32[2048,1024]{1,0:T(8,128)} %bitcast.135) | data formatting | bytes 16777216 | tf_op jit(solution)/shard_map/while/body/mul | solution.py:48
  137.8 4.3 mul.348
  142.0 9.2 %copy.46 = f32[2048,1024]{0,1:T(8,128)} copy(f32[2048,1024]{1,0:T(8,128)} %bitcast.136) | data formatting | bytes 16777216 | tf_op jit(solution)/shard_map/while/body/mul | solution.py:50
  151.2 12.0 %multiply_reduce_fusion.15 = (f32[2048]{0:T(1024)S(1)}, bf16[2048,1024]{0,1:T(8,128)(2,1)}) fusion(f32[2048,1024]{0,1:T(8,128)} %copy.45, f32[1024,2048]{1,0:T(8,128)} %copy-done, f32[2048,1024]{0,1:T(8,128)} %copy.46, f32[2048]{0:T(1024)S(1)} %get-tuple-element.938), kind=kLoop, calls=%fused_computation.19.clone.clone.1 | loop fusion | flops 16775168 | bytes 29376512 | tf_op jit(solution)/shard_map/while/body/reduce_sum | solution.py:48
  171.3 283.7 %while.34 = (s32[]{:T(128)}, f32[2048,128]{1,0:T(8,128)S(1)}, f32[64,32]{1,0:T(8,128)S(1)}, f32[4096,128]{1,0:T(8,128)}, s32[]{:T(128)}, /*index=5*/s32[]{:T(128...) while((s32[]{:T(128)}, f32[2048,128]{1,0:T(8,128)S(1)}, ...), condition=%wide.wide.region_3.4_spmd.clone, body=%wide.wide.region_0.3_spmd.clone.sunk | while | flops 1634472960 | bytes 194735712 | solution.py:120
  178.3 4.1 maximum_bitcast_fusion.7
  182.4 9.3 %copy.41 = f32[2048,1024]{1,0:T(8,128)} copy(f32[2048,1024]{0,1:T(8,128)} %maximum_bitcast_fusion.7) | data formatting | bytes 16777216 | tf_op jit(solution)/shard_map/while/body/max | solution.py:38
  191.7 4.8 multiply_reduce_fusion.12
  197.6 4.3 mul.334
  201.9 9.1 %copy.42 = f32[2048,1024]{0,1:T(8,128)} copy(f32[2048,1024]{1,0:T(8,128)} %bitcast.137) | data formatting | bytes 16777216 | tf_op jit(solution)/shard_map/while/body/mul | solution.py:48
  211.1 4.3 mul.335
  215.4 9.2 %copy.43 = f32[2048,1024]{0,1:T(8,128)} copy(f32[2048,1024]{1,0:T(8,128)} %bitcast.138) | data formatting | bytes 16777216 | tf_op jit(solution)/shard_map/while/body/mul | solution.py:50
  224.5 12.0 %multiply_reduce_fusion.13 = (f32[2048]{0:T(1024)S(1)}, bf16[2048,1024]{0,1:T(8,128)(2,1)}) fusion(f32[2048,1024]{0,1:T(8,128)} %copy.42, f32[1024,2048]{1,0:T(8,128)} %copy-done.1, f32[2048,1024]{0,1:T(8,128)} %copy.43, f32[2048]{0:T(1024)S(1)} %get-tuple-element.1016), kind=kLoop, calls=%fused_computation.2.clone.clone.1 | loop fusion | flops 16775168 | bytes 29376512 | tf_op jit(solution)/shard_map/while/body/reduce_sum | solution.py:48
  253.3 9.3 %copy.41 = f32[2048,1024]{1,0:T(8,128)} copy(f32[2048,1024]{0,1:T(8,128)} %maximum_bitcast_fusion.7) | data formatting | bytes 16777216 | tf_op jit(solution)/shard_map/while/body/max | solution.py:38
  262.6 4.8 multiply_reduce_fusion.12
  268.5 4.3 mul.334
  272.8 9.1 %copy.42 = f32[2048,1024]{0,1:T(8,128)} copy(f32[2048,1024]{1,0:T(8,128)} %bitcast.137) | data formatting | bytes 16777216 | tf_op jit(solution)/shard_map/while/body/mul | solution.py:48
  281.9 4.3 mul.335
  286.2 9.2 %copy.43 = f32[2048,1024]{0,1:T(8,128)} copy(f32[2048,1024]{1,0:T(8,128)} %bitcast.138) | data formatting | bytes 16777216 | tf_op jit(solution)/shard_map/while/body/mul | solution.py:50
  295.4 12.0 %multiply_reduce_fusion.13 = (f32[2048]{0:T(1024)S(1)}, bf16[2048,1024]{0,1:T(8,128)(2,1)}) fusion(f32[2048,1024]{0,1:T(8,128)} %copy.42, f32[1024,2048]{1,0:T(8,128)} %copy-done.1, f32[2048,1024]{0,1:T(8,128)} %copy.43, f32[2048]{0:T(1024)S(1)} %get-tuple-element.1016), kind=kLoop, calls=%fused_computation.2.clone.clone.1 | loop fusion | flops 16775168 | bytes 29376512 | tf_op jit(solution)/shard_map/while/body/reduce_sum | solution.py:48
  324.2 9.3 %copy.41 = f32[2048,1024]{1,0:T(8,128)} copy(f32[2048,1024]{0,1:T(8,128)} %maximum_bitcast_fusion.7) | data formatting | bytes 16777216 | tf_op jit(solution)/shard_map/while/body/max | solution.py:38
  333.5 4.8 multiply_reduce_fusion.12
  339.4 4.3 mul.334
  343.7 9.1 %copy.42 = f32[2048,1024]{0,1:T(8,128)} copy(f32[2048,1024]{1,0:T(8,128)} %bitcast.137) | data formatting | bytes 16777216 | tf_op jit(solution)/shard_map/while/body/mul | solution.py:48
  352.8 4.3 mul.335
  357.1 9.2 %copy.43 = f32[2048,1024]{0,1:T(8,128)} copy(f32[2048,1024]{1,0:T(8,128)} %bitcast.138) | data formatting | bytes 16777216 | tf_op jit(solution)/shard_map/while/body/mul | solution.py:50
  366.3 12.0 %multiply_reduce_fusion.13 = (f32[2048]{0:T(1024)S(1)}, bf16[2048,1024]{0,1:T(8,128)(2,1)}) fusion(f32[2048,1024]{0,1:T(8,128)} %copy.42, f32[1024,2048]{1,0:T(8,128)} %copy-done.1, f32[2048,1024]{0,1:T(8,128)} %copy.43, f32[2048]{0:T(1024)S(1)} %get-tuple-element.1016), kind=kLoop, calls=%fused_computation.2.clone.clone.1 | loop fusion | flops 16775168 | bytes 29376512 | tf_op jit(solution)/shard_map/while/body/reduce_sum | solution.py:48
  395.0 9.3 %copy.41 = f32[2048,1024]{1,0:T(8,128)} copy(f32[2048,1024]{0,1:T(8,128)} %maximum_bitcast_fusion.7) | data formatting | bytes 16777216 | tf_op jit(solution)/shard_map/while/body/max | solution.py:38
  404.3 4.8 multiply_reduce_fusion.12
  410.2 4.3 mul.334
  414.6 9.1 %copy.42 = f32[2048,1024]{0,1:T(8,128)} copy(f32[2048,1024]{1,0:T(8,128)} %bitcast.137) | data formatting | bytes 16777216 | tf_op jit(solution)/shard_map/while/body/mul | solution.py:48
  423.7 4.3 mul.335
  428.0 9.2 %copy.43 = f32[2048,1024]{0,1:T(8,128)} copy(f32[2048,1024]{1,0:T(8,128)} %bitcast.138) | data formatting | bytes 16777216 | tf_op jit(solution)/shard_map/while/body/mul | solution.py:50
  437.1 12.0 %multiply_reduce_fusion.13 = (f32[2048]{0:T(1024)S(1)}, bf16[2048,1024]{0,1:T(8,128)(2,1)}) fusion(f32[2048,1024]{0,1:T(8,128)} %copy.42, f32[1024,2048]{1,0:T(8,128)} %copy-done.1, f32[2048,1024]{0,1:T(8,128)} %copy.43, f32[2048]{0:T(1024)S(1)} %get-tuple-element.1016), kind=kLoop, calls=%fused_computation.2.clone.clone.1 | loop fusion | flops 16775168 | bytes 29376512 | tf_op jit(solution)/shard_map/while/body/reduce_sum | solution.py:48
  462.4 143.0 %collective-permute-start.1 = (bf16[3072,128]{1,0:T(8,128)(2,1)}, bf16[3072,128]{1,0:T(8,128)(2,1)}, u32[]{:S(2)}, u32[]{:S(2)}) collective-permute-start(bf16[3072,128]{1,0:T(8,128)(2,1)} %slice.88), channel_id=1, source_target_pairs={{1,0},{2,1},{3,2},{4,3},{5,4},{6,5},{7,6},{9,8},{10,9},{11,10},{12... | collective-permute-start | bytes 2359304 | tf_op jit(solution)/shard_map/ppermute | solution.py:15
  609.8 11.9 %collective-permute-done.1 = bf16[3072,128]{1,0:T(8,128)(2,1)} collective-permute-done((bf16[3072,128]{1,0:T(8,128)(2,1)}, bf16[3072,128]{1,0:T(8,128)(2,1)}, u32[]{:S(2)}, u32[]{:S(2)}) %collective-permute-start.1) | collective-permute-done | bytes 786464 | tf_op jit(solution)/shard_map/ppermute | solution.py:15
  (157 shorter events, 135.7 us)
Async XLA Ops:
  0.6 18.9 %copy-start.18 = (f32[1,2,64]{2,1,0:T(2,128)S(1)}, f32[1,2,64]{2,1,0:T(2,128)}, u32[]{:S(2)}) copy-start(f32[1,2,64]{2,1,0:T(2,128)} %param.17) | copy-start | bytes 1540
  0.6 18.9 %copy-start.17 = (f32[1,2,64]{2,1,0:T(2,128)S(1)}, f32[1,2,64]{2,1,0:T(2,128)}, u32[]{:S(2)}) copy-start(f32[1,2,64]{2,1,0:T(2,128)} %param.16) | copy-start | bytes 1540
  2.7 21.5 %collective-permute-start = (bf16[3072,128]{1,0:T(8,128)(2,1)}, bf16[3072,128]{1,0:T(8,128)(2,1)}, u32[]{:S(2)}, u32[]{:S(2)}) collective-permute-start(bf16[3072,128]{1,0:T(8,128)(2,1)} %slice_bitcast_fusion.1), channel_id=1, source_target_pairs={{0,1},{1,2},{2,3},{3,4},{4,5},{5,6},{6,7},{8,9},{9,10},{10,11},{11... | collective-permute-start | bytes 2359304 | tf_op jit(solution)/shard_map/ppermute | solution.py:15
  16.1 0.8 copy-start.12
  29.2 142.1 %copy-start.7 = (bf16[2048,128]{1,0:T(8,128)(2,1)S(1)}, bf16[2048,128]{1,0:T(8,128)(2,1)}, u32[]{:S(2)}) copy-start(bf16[2048,128]{1,0:T(8,128)(2,1)} %reshape_squeeze.6) | copy-start | bytes 1572868
  29.2 142.1 %copy-start.13 = (f32[1,1,64,32]{3,2,1,0:T(8,128)S(1)}, f32[1,1,64,32]{3,2,1,0:T(8,128)}, u32[]{:S(2)}) copy-start(f32[1,1,64,32]{3,2,1,0:T(8,128)} %copy-done.12) | copy-start | bytes 24580
  29.2 142.1 %copy-start.14 = (f32[2048]{0:T(1024)S(1)}, f32[2048]{0:T(1024)}, u32[]{:S(2)}) copy-start(f32[2048]{0:T(1024)} %mul.268) | copy-start | bytes 24580
  29.2 142.1 %copy-start.15 = (f32[1,1,64]{2,1,0:T(1,128)S(1)}, f32[1,1,64]{2,1,0:T(1,128)}, u32[]{:S(2)}) copy-start(f32[1,1,64]{2,1,0:T(1,128)} %get-tuple-element.961) | copy-start | bytes 772
  29.2 142.1 %copy-start.16 = (f32[1,1,64]{2,1,0:T(1,128)S(1)}, f32[1,1,64]{2,1,0:T(1,128)}, u32[]{:S(2)}) copy-start(f32[1,1,64]{2,1,0:T(1,128)} %get-tuple-element.959) | copy-start | bytes 772
  32.8 3.2 copy-start
  93.4 3.8 copy-start.2
  102.7 3.2 copy-start
  163.3 3.8 copy-start.2
  169.1 0.6 copy-start.10
  169.1 2.2 copy-start.4
  175.1 3.2 copy-start.1
  236.6 3.8 copy-start.3
  246.0 3.2 copy-start.1
  307.5 3.8 copy-start.3
  316.8 3.2 copy-start.1
  378.4 3.8 copy-start.3
  387.7 3.2 copy-start.1
  449.2 3.8 copy-start.3
  455.1 1.6 copy-start.9
  455.1 2.2 copy-start.8
  457.6 3.8 copy-start.6
  457.6 147.9 %copy-start.11 = (f32[64,32]{1,0:T(8,128)S(1)}, f32[64,32]{1,0:T(8,128)}, u32[]{:S(2)}) copy-start(f32[64,32]{1,0:T(8,128)} %copy-done.10) | copy-start | bytes 24580
  457.6 147.9 %copy-start.5 = (f32[2048,128]{1,0:T(8,128)S(1)}, f32[2048,128]{1,0:T(8,128)}, u32[]{:S(2)}) copy-start(f32[2048,128]{1,0:T(8,128)} %copy-done.4) | copy-start | bytes 3145732
  462.4 159.3 %collective-permute-start.1 = (bf16[3072,128]{1,0:T(8,128)(2,1)}, bf16[3072,128]{1,0:T(8,128)(2,1)}, u32[]{:S(2)}, u32[]{:S(2)}) collective-permute-start(bf16[3072,128]{1,0:T(8,128)(2,1)} %slice.88), channel_id=1, source_target_pairs={{1,0},{2,1},{3,2},{4,3},{5,4},{6,5},{7,6},{9,8},{10,9},{11,10},{12... | collective-permute-start | bytes 2359304 | tf_op jit(solution)/shard_map/ppermute | solution.py:15
where the time goes:
time: 631 us; the launch traced here: 625 us
  local copies, waits for them, and re-layouts  260 us (41%)
  other arithmetic  149 us (24%)
  starting transfers between devices  146 us (23%)
  matrix products  48 us (8%)
  waiting for transfers between devices  13.9 us (2%)
  between operations  7.39 us (1%)
    ppermute x2, starting transfers between devices, passed_along(): return lax.ppermute(array, axis, pairs)  146 us
    mul x12, local copies, waits for them, and re-layouts, block_terms(): delta[:, None, :] * weight_rows[:, :, None] * factor  80.8 us
    mul x12, local copies, waits for them, and re-layouts, block_terms(): weight_part = jnp.sum(delta[:, None, :] * active, axis=2)  80.6 us
    reduce_sum x6, other arithmetic, block_terms(): weight_part = jnp.sum(delta[:, None, :] * active, axis=2)  72 us
    max x6, local copies, waits for them, and re-layouts, block_terms(): active = jnp.maximum(scores, 0.0) * factor  55.8 us
    reduce_sum x6, other arithmetic, block_terms(): index_value = jnp.sum(weight_rows[:, :, None] * active, axis=1)  28.7 us
    max x6, other arithmetic, block_terms(): active = jnp.maximum(scores, 0.0) * factor  24.6 us
    dot_general x6, matrix products, block_terms(): jnp.dot(score_grad, key_block, preferred_element_type=jnp.float32)  22.5 us
  transfers between devices with their start and end apart: 2, of which 2 were waited for; matrix products, arithmetic and copies ran while one was open for 2% of the time, Pallas kernels for 0%

commit v1 on v0

v1 whole, which is shorter than its diff:
```python
import functools

import jax
import jax.numpy as jnp
from jax import lax
from jax.experimental import pallas as pl
from jax.experimental.pallas import tpu as pltpu
from jax.sharding import PartitionSpec as P

BLK = 1024
MAXB = 4
RIM = (MAXB - 1) * BLK
HALF = RIM // 2
WIDTH = 512
GROUP = 8
LANES = 128
DOWN = 2.0**-16
UP = 2.0**16
PRE_CHUNKS = 100
PIECE_CHUNKS = 0

f32 = jnp.float32
bf16 = jnp.bfloat16


def passed_along(array, by):
    size = lax.axis_size("ctx")
    pairs = [(i, i + by) for i in range(size) if 0 <= i + by < size]
    return lax.ppermute(array, "ctx", pairs)


def task_spans(slot_ref, doc_ref, tile_rows, regions):
    base = lax.axis_index("ctx") * (regions["own"][1] - RIM) - RIM
    tasks = []
    for i in range(doc_ref.shape[1]):
        doc = doc_ref[0, i] - base
        query = slot_ref[0, i] * tile_rows + RIM
        block = doc // BLK * BLK
        spans = {}
        for name, (start, stop) in regions.items():
            low = jnp.maximum(doc // LANES * LANES, start)
            high = jnp.minimum(query + tile_rows, stop)
            count = jnp.maximum(high - low + WIDTH - 1, 0) // WIDTH
            last = jnp.minimum(stop, block + MAXB * BLK) - WIDTH
            spans[name] = (low, count, last)
        tasks.append((doc, query, block, spans))
    return tasks


def pick(index, values):
    out = values[0]
    for i in range(1, len(values)):
        out = jnp.where(index == i, values[i], out)
    return out


def chunk_loop(tasks, name, begin, end, st):
    q2, wqt, wb, nm, ct, tg, keys, dq, dk, rb = st
    head_rows = q2.shape[1]
    tile_rows = nm.shape[1]
    rows = GROUP * tile_rows
    depth = q2.shape[2]
    lows = [t[3][name][0] for t in tasks]
    counts = [t[3][name][1] for t in tasks]
    lasts = [t[3][name][2] for t in tasks]
    factor = DOWN / depth**0.5

    def body(o, carry):
        task = jnp.int32(0)
        before = jnp.int32(0)
        seen = jnp.int32(0)
        for i in range(1, len(tasks)):
            seen = seen + counts[i - 1]
            task = jnp.where(o >= seen, i, task)
            before = jnp.where(o >= seen, seen, before)
        first = pick(task, lows) + (o - before) * WIDTH
        start = jnp.minimum(first, pick(task, lasts))
        start = pl.multiple_of(jnp.clip(start, 0, keys.shape[0] - WIDTH), LANES)
        column = start - pick(task, [t[2] for t in tasks])
        column = pl.multiple_of(jnp.clip(column, 0, tg.shape[2] - WIDTH), LANES)
        low = jnp.maximum(first, pick(task, [t[0] for t in tasks]))
        query = pick(task, [t[1] for t in tasks])
        span = pl.ds(start, WIDTH)
        key = keys[span, :]
        index = jnp.zeros((tile_rows, WIDTH), f32)
        for g in range(head_rows // rows):
            s = lax.dot_general(
                q2[task, g * rows : (g + 1) * rows, :],
                key,
                (((1,), (1,)), ((), ())),
                preferred_element_type=f32,
            )
            r = jnp.maximum(s, 0.0)
            for u in range(GROUP):
                w = wb[task, g * rows + u * tile_rows : g * rows + (u + 1) * tile_rows, :]
                w = jnp.concatenate([w] * (WIDTH // LANES), axis=1)
                index = index + w * r[u * tile_rows : (u + 1) * tile_rows]
            rb[g * rows : (g + 1) * rows, :] = r.astype(bf16)
        wide = [1, WIDTH // LANES]
        norm = jnp.concatenate([nm[task]] * wide[1], axis=1)
        cot = jnp.concatenate([ct[task]] * wide[1], axis=1)
        target = tg[task, :, pl.ds(column, WIDTH)].astype(f32)
        key_row = start + lax.broadcasted_iota(jnp.int32, (tile_rows, WIDTH), 1)
        query_row = query + lax.broadcasted_iota(jnp.int32, (tile_rows, WIDTH), 0)
        live = (key_row >= low) & (key_row <= query_row)
        delta = jnp.where(live, cot * (jnp.exp(index - norm) - target) * factor, 0.0)
        delta = jnp.concatenate([delta.astype(bf16)] * GROUP, axis=0)
        key_sum = None
        for g in range(head_rows // rows):
            here = slice(g * rows, (g + 1) * rows)
            grad = jnp.where(rb[here, :] > 0, delta, jnp.zeros_like(delta))
            dq[task, here, :] += jnp.dot(grad, key, preferred_element_type=f32)
            part = jnp.dot(wqt[task, :, here], grad, preferred_element_type=f32)
            key_sum = part if key_sum is None else key_sum + part
        dk[span, :] += key_sum.T
        return carry

    lax.fori_loop(begin, end, body, jnp.int32(0))


def own_share(tasks, stage):
    total = tasks[0][3]["own"][1]
    near = tasks[0][3]["near"][1]
    far = tasks[0][3]["far"][1]
    for t in tasks[1:]:
        total = total + t[3]["own"][1]
        near = near + t[3]["near"][1]
        far = far + t[3]["far"][1]
    one = jnp.minimum(total, PRE_CHUNKS)
    two = jnp.minimum(total, one + jnp.maximum(PIECE_CHUNKS - near, 0))
    three = jnp.minimum(total, two + jnp.maximum(PIECE_CHUNKS - far, 0))
    marks = [jnp.int32(0), one, two, three, total]
    return marks[stage], marks[stage + 1], near, far


def regions_of(own_rows):
    return {"far": (0, HALF), "near": (HALF, RIM), "own": (RIM, RIM + own_rows)}


def first_kernel(slot, doc, q, w, nrm, cot, tgt, key, q2, wqt, wb, nm, ct, tg, keys, dq, dk, rb, sems):
    own_rows = key.shape[1]
    copies = [
        pltpu.make_async_copy(key.at[0], keys.at[RIM : RIM + own_rows], sems.at[0]),
        pltpu.make_async_copy(tgt.at[0], tg, sems.at[1]),
    ]
    for copy in copies:
        copy.start()
    tile_rows = w.shape[2]
    heads = w.shape[3]
    depth = q2.shape[2]
    for i in range(w.shape[1]):
        weights = w[0, i] * (1.0 / depth**0.5)
        for h in range(heads):
            here = slice(h * tile_rows, (h + 1) * tile_rows)
            q2[i, here, :] = q[0, i, :, h * depth : (h + 1) * depth]
            wb[i, here, :] = jnp.broadcast_to(weights[:, h : h + 1], (tile_rows, LANES))
        for h in range(0, heads, 2):
            here = slice(h * tile_rows, (h + 2) * tile_rows)
            wide = jnp.concatenate(
                [jnp.broadcast_to(w[0, i, :, u : u + 1], (tile_rows, depth)) for u in (h, h + 1)], axis=0
            )
            wqt[i, :, here] = (q2[i, here, :].astype(f32) * wide).T.astype(bf16)
        nm[i] = jnp.broadcast_to(nrm[0, i : i + 1, :], (LANES, tile_rows)).T
        ct[i] = jnp.broadcast_to(cot[0, i : i + 1, :], (LANES, tile_rows)).T
    dq[...] = jnp.zeros_like(dq)
    dk[...] = jnp.zeros_like(dk)
    for copy in copies:
        copy.wait()
    tasks = task_spans(slot, doc, tile_rows, regions_of(own_rows))
    begin, end, _, _ = own_share(tasks, 0)
    chunk_loop(tasks, "own", begin, end, (q2, wqt, wb, nm, ct, tg, keys, dq, dk, rb))


def piece_kernel(name, slot, doc, rim, q2, wqt, wb, nm, ct, tg, *refs):
    keys, dq, dk, lent, rb = refs[3:]
    tile_rows = nm.shape[1]
    own_rows = keys.shape[0] - RIM
    regions = regions_of(own_rows)
    start, stop = regions[name]
    keys[start:stop, :] = rim[...]
    tasks = task_spans(slot, doc, tile_rows, regions)
    begin, end, near, far = own_share(tasks, 1 if name == "near" else 2)
    st = (q2, wqt, wb, nm, ct, tg, keys, dq, dk, rb)
    chunk_loop(tasks, name, 0, near if name == "near" else far, st)
    lent[...] = (dk[start:stop, :] * UP).astype(bf16)
    chunk_loop(tasks, "own", begin, end, st)


def last_kernel(slot, doc, q2, wqt, wb, nm, ct, tg, keys, dq, dk_in, dk, q_out, w_out, k_out, rb):
    tile_rows = nm.shape[1]
    depth = q2.shape[2]
    own_rows = keys.shape[0] - RIM
    tasks = task_spans(slot, doc, tile_rows, regions_of(own_rows))
    begin, end, _, _ = own_share(tasks, 3)
    chunk_loop(tasks, "own", begin, end, (q2, wqt, wb, nm, ct, tg, keys, dq, dk, rb))
    for i in range(q2.shape[0]):
        for h in range(q2.shape[1] // tile_rows):
            here = slice(h * tile_rows, (h + 1) * tile_rows)
            grad = dq[i, here, :]
            q_out[0, i, :, h * depth : (h + 1) * depth] = (
                grad * (wb[i, here, :] * (UP * depth**0.5))
            ).astype(bf16)
            w_out[0, i, :, h : h + 1] = UP * jnp.sum(
                grad * q2[i, here, :].astype(f32), axis=1, keepdims=True
            )
    k_out[0] = (dk[RIM:, :] * UP).astype(bf16)


def add_kernel(k_in, dk, near, far, k_out, tail, sem):
    own_rows = k_out.shape[1]
    own = dk[RIM + own_rows - RIM :, :] * UP
    tail[:HALF] = (own[:HALF] + far[...].astype(f32)).astype(bf16)
    tail[HALF:] = (own[HALF:] + near[...].astype(f32)).astype(bf16)
    copy = pltpu.make_async_copy(tail, k_out.at[0, own_rows - RIM :], sem)
    copy.start()
    copy.wait()


def local(queries, head_weights, key_vectors, targets, normalizers, loss_grad, tile_slot, doc_start):
    task_count, tile_rows, width = queries.shape[1:]
    heads = head_weights.shape[3]
    own_rows, depth = key_vectors.shape[1:]
    head_rows = heads * tile_rows
    vmem = pl.BlockSpec(memory_space=pltpu.VMEM)
    smem = pl.BlockSpec(memory_space=pltpu.SMEM)
    anywhere = pl.BlockSpec(memory_space=pl.ANY)
    params = pltpu.CompilerParams(vmem_limit_bytes=40 * 2**20)
    hold = lambda shape, kind: pltpu.VMEM(shape, kind)
    keep = lambda x: pltpu.with_memory_space_constraint(x, pltpu.VMEM)

    far_keys = passed_along(key_vectors[0, own_rows - RIM : own_rows - HALF], 1)
    near_keys = passed_along(key_vectors[0, own_rows - HALF :], 1)
    scratch = pltpu.VMEM((head_rows, WIDTH), bf16)
    state = [
        hold((task_count, head_rows, depth), bf16),
        hold((task_count, depth, head_rows), bf16),
        hold((task_count, head_rows, LANES), f32),
        hold((task_count, tile_rows, LANES), f32),
        hold((task_count, tile_rows, LANES), f32),
        hold(targets.shape[1:], bf16),
        hold((RIM + own_rows, depth), bf16),
        hold((task_count, head_rows, depth), f32),
        hold((RIM + own_rows, depth), f32),
    ]
    st = pl.pallas_call(
        first_kernel,
        in_specs=[smem, smem, vmem, vmem, vmem, vmem, anywhere, anywhere],
        out_specs=[vmem] * 9,
        out_shape=state,
        scratch_shapes=[scratch, pltpu.SemaphoreType.DMA((2,))],
        compiler_params=params,
        name="own_first",
    )(tile_slot, doc_start, queries, head_weights, normalizers, loss_grad, targets, key_vectors)
    fixed, moving = st[:6], st[6:]

    def piece(name, rim, moving):
        out = pl.pallas_call(
            functools.partial(piece_kernel, name),
            in_specs=[smem, smem] + [vmem] * 10,
            out_specs=[vmem] * 4,
            out_shape=state[6:] + [hold(rim.shape, bf16)],
            input_output_aliases={9: 0, 10: 1, 11: 2},
            scratch_shapes=[scratch],
            compiler_params=params,
            name="borrowed_" + name,
        )(tile_slot, doc_start, rim, *[keep(x) for x in fixed], *[keep(x) for x in moving])
        return out[:3], out[3]

    moving, near_lent = piece("near", near_keys, moving)
    near_back = passed_along(near_lent, -1)
    moving, far_lent = piece("far", far_keys, moving)
    far_back = passed_along(far_lent, -1)
    dk, q_out, w_out, k_out = pl.pallas_call(
        last_kernel,
        in_specs=[smem, smem] + [vmem] * 9,
        out_specs=[vmem] * 4,
        out_shape=[
            state[8],
            jax.ShapeDtypeStruct(queries.shape, bf16),
            jax.ShapeDtypeStruct(head_weights.shape, f32),
            jax.ShapeDtypeStruct(key_vectors.shape, bf16),
        ],
        input_output_aliases={10: 0},
        scratch_shapes=[scratch],
        compiler_params=params,
        name="own_last",
    )(tile_slot, doc_start, *[keep(x) for x in fixed], *[keep(x) for x in moving])
    k_out = pl.pallas_call(
        add_kernel,
        in_specs=[anywhere, vmem, vmem, vmem],
        out_specs=anywhere,
        out_shape=jax.ShapeDtypeStruct(key_vectors.shape, bf16),
        input_output_aliases={0: 0},
        scratch_shapes=[pltpu.VMEM((RIM, depth), bf16), pltpu.SemaphoreType.DMA],
        compiler_params=params,
        name="add_lent",
    )(k_out, keep(dk), near_back, far_back)
    return q_out, w_out, k_out


def solution(mesh):
    return jax.shard_map(
        local,
        mesh=mesh,
        in_specs=(
            P("sec", "ctx", None, None),
            P("sec", "ctx", None, None),
            P("sec", "ctx", None),
            P("sec", "ctx", None, None),
            P("sec", "ctx", None),
            P("sec", "ctx", None),
            P("sec", "ctx"),
            P("sec", "ctx"),
        ),
        out_specs=(P("sec", "ctx", None, None), P("sec", "ctx", None, None), P("sec", "ctx", None)),
        check_vma=False,
    )
```

time: 631 us -> 68.4 us (0.11)
  the two profiles are of different devices: /device:TPU:22 before, /device:TPU:7 now
where the time goes in v1:
time: 68.4 us; the launch traced here: 67.7 us
  Pallas kernels  36.4 us (53%)
  local copies, waits for them, and re-layouts  10.8 us (16%)
  starting transfers between devices  10.1 us (15%)
  waiting for transfers between devices  9.58 us (14%)
  between operations  0.89 us (1%)
    pallas_call x1, Pallas kernels, local(): pl.pallas_call(first_kernel, in_specs=[smem, smem, vmem, vmem, vmem, vmem...  24.3 us
    ppermute x4, starting transfers between devices, passed_along(): return lax.ppermute(array, 'ctx', pairs)  10.1 us
    unnamed x10, local copies, waits for them, and re-layouts  9.58 us
    ppermute x4, waiting for transfers between devices, passed_along(): return lax.ppermute(array, 'ctx', pairs)  9.58 us
    pallas_call x2, Pallas kernels, piece(): pl.pallas_call(functools.partial(piece_kernel, name), in_specs=[smem, sme...  7.68 us
    pallas_call x1, Pallas kernels, local(): pl.pallas_call(last_kernel, in_specs=[smem, smem] + [vmem] * 9, out_specs...  3.34 us
  transfers between devices with their start and end apart: 4, of which 2 were waited for; matrix products, arithmetic and copies ran while one was open for 4% of the time, Pallas kernels for 51%

profile of v1, /device:TPU:7, one launch (start us, length us, event | category | flops | bytes accessed | tf_op | source)
XLA Modules:
  0.0 67.7 jit_solution(2027325917308790591)
XLA Ops:
  0.6 1.2 %slice_bitcast_fusion = (bf16[1536,128]{1,0:T(8,128)(2,1)S(1)}, bf16[1536,128]{1,0:T(8,128)(2,1)S(1)}) fusion(bf16[1,8192,128]{2,1,0:T(8,128)(2,1)} %key.1), kind=kLoop, calls=%fused_computation | loop fusion | bytes 1572864 | tf_op jit(solution)/shard_map/squeeze | solution.py:232
  1.8 3.1 %collective-permute-start.1 = (bf16[1536,128]{1,0:T(8,128)(2,1)S(1)}, bf16[1536,128]{1,0:T(8,128)(2,1)S(1)}, u32[]{:S(2)}, u32[]{:S(2)}) collective-permute-start(bf16[1536,128]{1,0:T(8,128)(2,1)S(1)} %get-tuple-element.48), channel_id=1, source_target_pairs={{0,1},{1,2},{2,3},{3,4},{4,5},{5,6},{6,7},{8,9},{9,10},{10,11},{11... | collective-permute-start | bytes 1179656 | tf_op jit(solution)/shard_map/ppermute | solution.py:29
  5.0 3.1 %collective-permute-start = (bf16[1536,128]{1,0:T(8,128)(2,1)S(1)}, bf16[1536,128]{1,0:T(8,128)(2,1)S(1)}, u32[]{:S(2)}, u32[]{:S(2)}) collective-permute-start(bf16[1536,128]{1,0:T(8,128)(2,1)S(1)} %get-tuple-element.49), channel_id=1, source_target_pairs={{0,1},{1,2},{2,3},{3,4},{4,5},{5,6},{6,7},{8,9},{9,10},{10,11},{11... | collective-permute-start | bytes 1179656 | tf_op jit(solution)/shard_map/ppermute | solution.py:29
  8.1 1.5 %copy.19.w = f32[1,2,64,32]{3,2,1,0:T(8,128)} copy(f32[1,2,64,32]{2,3,1,0:T(8,128)} %param.9) | data formatting | bytes 32768 | tf_op args[1]
  9.6 24.3 %own_first.1 = (bf16[2,2048,128]{2,1,0:T(8,128)(2,1)S(1)}, bf16[2,128,2048]{2,1,0:T(8,128)(2,1)S(1)}, f32[2,2048,128]{2,1,0:T(8,128)S(1)}, f32[2,64,128]{2,1,0:T...) custom-call(s32[1,2]{1,0:T(1,128)} %slot.7, ...), custom_call_target="tpu_custom_call" | custom-call | tf_op jit(solution)/shard_map/own_first/pallas_call | solution.py:245
  33.9 0.0 collective-permute-done.1.rim
  33.9 0.0 copy-start.3
  33.9 0.7 %copy-done.3 = bf16[1536,128]{1,0:T(8,128)(2,1)} copy-done((bf16[1536,128]{1,0:T(8,128)(2,1)}, bf16[1536,128]{1,0:T(8,128)(2,1)S(1)}, u32[]{:S(2)}) %copy-start.3) | copy-done | bytes 393240
  34.6 6.6 %borrowed_near.1 = (bf16[11264,128]{1,0:T(8,128)(2,1)S(1)}, f32[2,2048,128]{2,1,0:T(8,128)S(1)}, f32[11264,128]{1,0:T(8,128)S(1)}, bf16[1536,128]{1,0:T(8,128)(2,1)S(1)}) custom-call(s32[1,2]{1,0:T(1,128)} %slot.7, s32[1,2]{1,0:T(1,128)} %doc.7, bf16[1536,128]{1,0:T(8,128)(2,1)} %copy-done.3, ...), custom_call_target="tpu_custom_call", output_to_operand_aliasing={{0}: (9, {}), {1}: (10, {}), {2}: (11, {})} | custom-call | tf_op jit(solution)/shard_map/borrowed_near/pallas_call | solution.py:257
  41.2 0.0 collective-permute-done.rim
  41.2 0.0 copy-start.2
  41.2 0.7 %copy-done.2 = bf16[1536,128]{1,0:T(8,128)(2,1)} copy-done((bf16[1536,128]{1,0:T(8,128)(2,1)}, bf16[1536,128]{1,0:T(8,128)(2,1)S(1)}, u32[]{:S(2)}) %copy-start.2) | copy-done | bytes 393240
  42.0 1.1 %borrowed_far.1 = (bf16[11264,128]{1,0:T(8,128)(2,1)S(1)}, f32[2,2048,128]{2,1,0:T(8,128)S(1)}, f32[11264,128]{1,0:T(8,128)S(1)}, bf16[1536,128]{1,0:T(8,128)(2,1)S(1)}) custom-call(s32[1,2]{1,0:T(1,128)} %slot.7, s32[1,2]{1,0:T(1,128)} %doc.7, bf16[1536,128]{1,0:T(8,128)(2,1)} %copy-done.2, ...), custom_call_target="tpu_custom_call", output_to_operand_aliasing={{0}: (9, {}), {1}: (10, {}), {2}: (11, {})} | custom-call | tf_op jit(solution)/shard_map/borrowed_far/pallas_call | solution.py:257
  43.1 1.9 %collective-permute-start.3 = (bf16[1536,128]{1,0:T(8,128)(2,1)S(1)}, bf16[1536,128]{1,0:T(8,128)(2,1)S(1)}, u32[]{:S(2)}, u32[]{:S(2)}) collective-permute-start(bf16[1536,128]{1,0:T(8,128)(2,1)S(1)} %get-tuple-element.44), channel_id=1, source_target_pairs={{1,0},{2,1},{3,2},{4,3},{5,4},{6,5},{7,6},{9,8},{10,9},{11,10},{12... | collective-permute-start | bytes 1179656 | tf_op jit(solution)/shard_map/ppermute | solution.py:29
  45.0 1.9 %collective-permute-start.2 = (bf16[1536,128]{1,0:T(8,128)(2,1)S(1)}, bf16[1536,128]{1,0:T(8,128)(2,1)S(1)}, u32[]{:S(2)}, u32[]{:S(2)}) collective-permute-start(bf16[1536,128]{1,0:T(8,128)(2,1)S(1)} %get-tuple-element.43), channel_id=1, source_target_pairs={{1,0},{2,1},{3,2},{4,3},{5,4},{6,5},{7,6},{9,8},{10,9},{11,10},{12... | collective-permute-start | bytes 1179656 | tf_op jit(solution)/shard_map/ppermute | solution.py:29
  47.0 3.3 %own_last.1 = (f32[11264,128]{1,0:T(8,128)S(1)}, bf16[1,2,64,4096]{3,2,1,0:T(8,128)(2,1)}, f32[1,2,64,32]{3,2,1,0:T(8,128)}, bf16[1,8192,128]{2,1,0:T(8,128)(2,1)}) custom-call(s32[1,2]{1,0:T(1,128)} %slot.7, s32[1,2]{1,0:T(1,128)} %doc.7, bf16[2,2048,128]{2,1,0:T(8,128)(2,1)S(1)} %get-tuple-element.24.q2, ...), custom_call_target="tpu_custom_call", output_to_operand_aliasing={{0}: (10, {})} | custom-call | tf_op jit(solution)/shard_map/own_last/pallas_call | solution.py:273
  50.3 0.0 copy-start
  50.3 2.5 %copy-done = f32[11264,128]{1,0:T(8,128)} copy-done((f32[11264,128]{1,0:T(8,128)}, f32[11264,128]{1,0:T(8,128)S(1)}, u32[]{:S(2)}) %copy-start) | copy-done | bytes 5767192
  52.8 1.5 %copy.20 = f32[1,2,64,32]{2,3,1,0:T(8,128)} copy(f32[1,2,64,32]{3,2,1,0:T(8,128)} %get-tuple-element.46) | data formatting | bytes 32768
  54.3 1.1 %collective-permute-done.3.far = bf16[1536,128]{1,0:T(8,128)(2,1)S(1)} collective-permute-done((bf16[1536,128]{1,0:T(8,128)(2,1)S(1)}, bf16[1536,128]{1,0:T(8,128)(2,1)S(1)}, u32[]{:S(2)}, u32[]{:S(2)}) %collective-permute-start.3) | collective-permute-done | bytes 393248 | tf_op jit(solution)/shard_map/ppermute | solution.py:29
  55.4 8.4 %collective-permute-done.2.near = bf16[1536,128]{1,0:T(8,128)(2,1)S(1)} collective-permute-done((bf16[1536,128]{1,0:T(8,128)(2,1)S(1)}, bf16[1536,128]{1,0:T(8,128)(2,1)S(1)}, u32[]{:S(2)}, u32[]{:S(2)}) %collective-permute-start.2) | collective-permute-done | bytes 393248 | tf_op jit(solution)/shard_map/ppermute | solution.py:29
  63.9 0.0 copy-start.1
  63.9 2.6 %copy-done.1 = f32[11264,128]{1,0:T(8,128)S(1)} copy-done((f32[11264,128]{1,0:T(8,128)S(1)}, f32[11264,128]{1,0:T(8,128)}, u32[]{:S(2)}) %copy-start.1) | copy-done | bytes 5767192
  66.5 1.1 %add_lent.1 = bf16[1,8192,128]{2,1,0:T(8,128)(2,1)} custom-call(bf16[1,8192,128]{2,1,0:T(8,128)(2,1)} %get-tuple-element.41.k_in, f32[11264,128]{1,0:T(8,128)S(1)} %copy-done.1, bf16[1536,128]{1,0:T(8,128)(2,1)S(1)} %collective-permute-done.2.near, bf16[1536,128]{1,0:T(8,128)(2,1)S(1)} %collective-permute-done.3.far), custom_call_target="tpu_custom_call", output_to_operand_aliasing={{}: (0, {})} | custom-call | tf_op jit(solution)/shard_map/add_lent/pallas_call | solution.py:288
Async XLA Ops:
  1.8 32.1 %collective-permute-start.1 = (bf16[1536,128]{1,0:T(8,128)(2,1)S(1)}, bf16[1536,128]{1,0:T(8,128)(2,1)S(1)}, u32[]{:S(2)}, u32[]{:S(2)}) collective-permute-start(bf16[1536,128]{1,0:T(8,128)(2,1)S(1)} %get-tuple-element.48), channel_id=1, source_target_pairs={{0,1},{1,2},{2,3},{3,4},{4,5},{5,6},{6,7},{8,9},{9,10},{10,11},{11... | collective-permute-start | bytes 1179656 | tf_op jit(solution)/shard_map/ppermute | solution.py:29
  5.0 36.3 %collective-permute-start = (bf16[1536,128]{1,0:T(8,128)(2,1)S(1)}, bf16[1536,128]{1,0:T(8,128)(2,1)S(1)}, u32[]{:S(2)}, u32[]{:S(2)}) collective-permute-start(bf16[1536,128]{1,0:T(8,128)(2,1)S(1)} %get-tuple-element.49), channel_id=1, source_target_pairs={{0,1},{1,2},{2,3},{3,4},{4,5},{5,6},{6,7},{8,9},{9,10},{10,11},{11... | collective-permute-start | bytes 1179656 | tf_op jit(solution)/shard_map/ppermute | solution.py:29
  33.9 0.7 %copy-start.3 = (bf16[1536,128]{1,0:T(8,128)(2,1)}, bf16[1536,128]{1,0:T(8,128)(2,1)S(1)}, u32[]{:S(2)}) copy-start(bf16[1536,128]{1,0:T(8,128)(2,1)S(1)} %collective-permute-done.1.rim) | copy-start | bytes 1179652
  41.2 0.7 %copy-start.2 = (bf16[1536,128]{1,0:T(8,128)(2,1)}, bf16[1536,128]{1,0:T(8,128)(2,1)S(1)}, u32[]{:S(2)}) copy-start(bf16[1536,128]{1,0:T(8,128)(2,1)S(1)} %collective-permute-done.rim) | copy-start | bytes 1179652
  43.1 12.3 %collective-permute-start.3 = (bf16[1536,128]{1,0:T(8,128)(2,1)S(1)}, bf16[1536,128]{1,0:T(8,128)(2,1)S(1)}, u32[]{:S(2)}, u32[]{:S(2)}) collective-permute-start(bf16[1536,128]{1,0:T(8,128)(2,1)S(1)} %get-tuple-element.44), channel_id=1, source_target_pairs={{1,0},{2,1},{3,2},{4,3},{5,4},{6,5},{7,6},{9,8},{10,9},{11,10},{12... | collective-permute-start | bytes 1179656 | tf_op jit(solution)/shard_map/ppermute | solution.py:29
  45.0 18.8 %collective-permute-start.2 = (bf16[1536,128]{1,0:T(8,128)(2,1)S(1)}, bf16[1536,128]{1,0:T(8,128)(2,1)S(1)}, u32[]{:S(2)}, u32[]{:S(2)}) collective-permute-start(bf16[1536,128]{1,0:T(8,128)(2,1)S(1)} %get-tuple-element.43), channel_id=1, source_target_pairs={{1,0},{2,1},{3,2},{4,3},{5,4},{6,5},{7,6},{9,8},{10,9},{11,10},{12... | collective-permute-start | bytes 1179656 | tf_op jit(solution)/shard_map/ppermute | solution.py:29
  50.3 2.5 %copy-start = (f32[11264,128]{1,0:T(8,128)}, f32[11264,128]{1,0:T(8,128)S(1)}, u32[]{:S(2)}) copy-start(f32[11264,128]{1,0:T(8,128)S(1)} %get-tuple-element.42.dk) | copy-start | bytes 17301508
  63.9 2.6 %copy-start.1 = (f32[11264,128]{1,0:T(8,128)S(1)}, f32[11264,128]{1,0:T(8,128)}, u32[]{:S(2)}) copy-start(f32[11264,128]{1,0:T(8,128)} %copy-done) | copy-start | bytes 17301508
